TPU v7x, 32 devices: a whole 2x2x4 slice. The times are simulated.
32 devices in a mesh: pole: 2 (over core), row: 2 (over y), col: 2 (over x), layer: 4 (over z).
Axes of the slice: x: 2, y: 2, z: 4, core: 2. Of those that a mesh axis runs over, the one named last changes fastest.
Arguments:
- hamilton: bfloat16 [1024, 1024], P('layer', ('row', 'col')), may hold values from -0.005859375 to 0.005859375
- intersection: bfloat16 [1024, 1024], P('layer', ('row', 'col')), may hold values from -0.005859375 to 0.005859375
- guess: bfloat16 [2, 2, 1024, 1024], P('pole', None, 'layer', ('row', 'col')), may hold values from -6 to 6
- poles: float32 [2, 2], P('pole'), may hold values from -1.5 to 1.5
- weights: float32 [2, 2], P('pole'), may hold values from -1 to 1
- keep: int32 [2, 8, 8], P('pole'), may hold values from 0 to 1, as said below
Outputs:
- density: float32 [4, 2, 128, 1024], P('layer', 'pole', None, ('row', 'col'))
Inputs may be any that keep to these rules, and one draw needn't show every extreme that they name: keep[p, i, j] is 1 where tile (i, j) survives pole p's filter and 0 where it is dropped; diagonal tiles are always kept.
All inputs are finite; a program needn't handle non-finite values.
Results may differ from a plain program's by a relative error of at most 0.0032.
Values may be sent and summed in bfloat16 or wider, within the bound.
A program may use at most 64 MiB of HBM per device.

v0:
```python
import jax
import jax.numpy as jnp
from jax import lax
from jax.sharding import PartitionSpec as P

BLOCK = 128


def tile_mask(keep_float, row_ids, col_ids):
    tile_count = keep_float.shape[0]
    tile_ids = jnp.arange(tile_count, dtype=jnp.int32)
    pick_rows = (row_ids[:, None] // BLOCK == tile_ids[None, :]).astype(jnp.float32)
    pick_cols = (col_ids[:, None] // BLOCK == tile_ids[None, :]).astype(jnp.float32)
    half_mask = jnp.dot(pick_rows, keep_float, precision=lax.Precision.HIGHEST)
    return jnp.dot(half_mask, pick_cols.T, precision=lax.Precision.HIGHEST)


def fold_terms(left_panel, piece):
    real_part = jnp.dot(left_panel[0], piece[0], preferred_element_type=jnp.float32) - jnp.dot(
        left_panel[1], piece[1], preferred_element_type=jnp.float32
    )
    imag_part = jnp.dot(left_panel[0], piece[1], preferred_element_type=jnp.float32) + jnp.dot(
        left_panel[1], piece[0], preferred_element_type=jnp.float32
    )
    return jnp.stack([real_part, imag_part])


def per_device(hamilton, intersection, guess, poles, weights, keep):
    rows_local, cols_local = hamilton.shape
    layer_index = lax.axis_index("layer")
    span_index = lax.axis_index("row") * lax.axis_size("col") + lax.axis_index("col")
    row_ids = layer_index * rows_local + jnp.arange(rows_local, dtype=jnp.int32)
    col_ids = span_index * cols_local + jnp.arange(cols_local, dtype=jnp.int32)
    ham_rows, ovl_rows = (
        lax.all_gather(hamilton, ("row", "col"), axis=1, tiled=True),
        lax.all_gather(intersection, ("row", "col"), axis=1, tiled=True),
    )
    ham_wide = ham_rows.astype(jnp.float32)
    ovl_wide = ovl_rows.astype(jnp.float32)
    real_pole = poles[0, 0]
    imag_pole = poles[0, 1]
    system_panel = jnp.stack([real_pole * ovl_wide - ham_wide, imag_pole * ovl_wide]).astype(
        jnp.bfloat16
    )
    guess_local = guess[0]
    own_mask = tile_mask(keep[0].astype(jnp.float32), row_ids, col_ids)
    first = fold_terms(system_panel, lax.all_gather(guess_local, "layer", axis=1, tiled=True))
    product_local = (own_mask[None] * first).astype(jnp.bfloat16)
    guess_panel = lax.all_gather(guess_local, ("row", "col"), axis=2, tiled=True)
    back = fold_terms(guess_panel, lax.all_gather(product_local, "layer", axis=1, tiled=True))
    refined = own_mask[None] * (2.0 * guess_local.astype(jnp.float32) - back)
    contrib = weights[0, 0] * refined[0] - weights[0, 1] * refined[1]
    reduced = lax.psum_scatter(contrib, "pole", scatter_dimension=0, tiled=True)
    return reduced.reshape(1, 1, reduced.shape[0], cols_local)


def solution(mesh):
    in_specs = (
        P("layer", ("row", "col")),
        P("layer", ("row", "col")),
        P("pole", None, "layer", ("row", "col")),
        P("pole", None),
        P("pole", None),
        P("pole", None, None),
    )
    out_specs = P("layer", "pole", None, ("row", "col"))
    return jax.shard_map(
        per_device, mesh=mesh, in_specs=in_specs, out_specs=out_specs, check_vma=False
    )
```

profile of v0, /device:TPU:0, one launch (start us, length us, event | category | flops | bytes accessed | tf_op | source)
XLA Modules:
  0.0 117.2 jit_solution(15884552957494208425)
XLA Ops:
  6.5 0.7 all-gather.8.cloned.1.call-update
  7.3 0.0 all-gather.10.cloned.1.call-start
  7.3 0.7 all-gather.10.cloned.1.call-update
  8.0 0.0 all-gather.6.cloned.1.call-start
  8.1 0.1 copy-done.1
  8.2 15.1 %all_gather.15 = bf16[256,1024]{1,0:T(8,128)(2,1)S(1)} all-gather(bf16[256,256]{1,0:T(8,128)(2,1)S(1)} %copy-done.1), channel_id=1, replica_groups=mesh['pole'=2,'row'=2,'col'=2,'layer'=4] {'row','col'}, dimensions={1}, use_global_device_ids=true | all-gather | bytes 655360 | tf_op jit(solution)/shard_map/all_gather | solution.py:36
  23.2 0.6 fusion.26
  23.8 12.1 %all_gather.16 = bf16[256,1024]{1,0:T(8,128)(2,1)S(1)} all-gather(bf16[256,256]{1,0:T(8,128)(2,1)S(1)} %copy-done.2), channel_id=1, replica_groups=mesh['pole'=2,'row'=2,'col'=2,'layer'=4] {'row','col'}, dimensions={1}, use_global_device_ids=true | all-gather | bytes 655360 | tf_op jit(solution)/shard_map/all_gather | solution.py:35
  36.0 0.7 copy-done.3
  36.6 0.3 fusion.19
  36.9 0.3 fusion.20
  37.2 2.4 %all-gather.8.cloned.1.call-done = bf16[1,2,1024,256]{3,2,1,0:T(8,128)(2,1)} async-done(((bf16[1,2,256,256]{3,2,1,0:T(8,128)(2,1)}), bf16[1,2,1024,256]{3,2,1,0:T(8,128)(2,1)}) %all-gather.8.cloned.1.call-update) | async-done | bytes 1048592 | tf_op jit(solution)/shard_map/all_gather | solution.py:47
  39.6 2.0 %fusion.11 = f32[256,256]{1,0:T(8,128)S(1)} fusion(bf16[1,2,1024,256]{3,2,1,0:T(8,128)(2,1)} %all-gather.8.cloned.1.call-done, bf16[256,1024]{1,0:T(8,128)(2,1)S(1)} %all_gather.15, bf16[256,1024]{1,0:T(8,128)(2,1)S(1)} %all_gather.16, f32[]{:T(128)} %bitcast.3), kind=kOutput, calls=%fused_computation.25 | convolution fusion | flops 135528448 | bytes 1835520 | tf_op jit(solution)/shard_map/dot_general | solution.py:19
  41.6 1.0 fusion.3
  42.6 0.9 fusion.12
  43.5 1.0 fusion.2
  44.5 0.8 fusion.7
  45.2 0.0 all-gather.6.cloned.1.call-update
  45.2 0.0 reduce-scatter.2.cloned.1.call-start
  45.3 0.6 copy-done.5
  45.9 0.7 fusion.25
  46.5 20.9 %all-gather.10.cloned.1.call-done = bf16[1,2,256,1024]{3,2,1,0:T(8,128)(2,1)} async-done(((bf16[1,2,256,256]{3,2,1,0:T(8,128)(2,1)}), bf16[1,2,256,1024]{3,2,1,0:T(8,128)(2,1)}) %all-gather.10.cloned.1.call-update) | async-done | bytes 1048592 | tf_op jit(solution)/shard_map/all_gather | solution.py:49
  67.4 29.5 %all-gather.6.cloned.1.call-done = bf16[2,1024,256]{2,1,0:T(8,128)(2,1)} async-done(((bf16[2,256,256]{2,1,0:T(8,128)(2,1)}), bf16[2,1024,256]{2,1,0:T(8,128)(2,1)}) %all-gather.6.cloned.1.call-update) | async-done | bytes 1048592 | tf_op jit(solution)/shard_map/all_gather | solution.py:50
  97.0 1.5 %fusion.9 = f32[256,256]{0,1:T(8,128)S(1)} fusion(bf16[1,2,256,1024]{3,2,1,0:T(8,128)(2,1)} %all-gather.10.cloned.1.call-done, bf16[2,1024,256]{2,1,0:T(8,128)(2,1)} %all-gather.6.cloned.1.call-done), kind=kOutput, calls=%fused_computation.23 | convolution fusion | flops 134217728 | bytes 1310720 | tf_op jit(solution)/shard_map/dot_general | solution.py:19
  98.5 1.4 %fusion.10 = f32[256,256]{0,1:T(8,128)S(1)} fusion(bf16[1,2,256,1024]{3,2,1,0:T(8,128)(2,1)S(1)} %copy-done.6, bf16[2,1024,256]{2,1,0:T(8,128)(2,1)} %all-gather.6.cloned.1.call-done), kind=kOutput, calls=%fused_computation.24 | convolution fusion | flops 134217728 | bytes 1310720 | tf_op jit(solution)/shard_map/dot_general | solution.py:22
  100.0 0.3 fusion.1
  100.3 0.3 fusion
  100.6 0.6 copy-done
  101.2 0.1 fusion.8
  101.3 2.1 %fusion.16 = f32[256,256]{1,0:T(8,128)} fusion(f32[2,256,256]{2,1,0:T(8,128)S(1)} %fusion.8, f32[]{:T(128)} %bitcast.17, f32[]{:T(128)} %bitcast), kind=kLoop, calls=%fused_computation.29 | loop fusion | flops 196608 | bytes 786440 | tf_op jit(solution)/shard_map/sub | solution.py:52
  103.4 0.0 reduce-scatter.2.cloned.1.call-update
  103.4 7.3 %reduce-scatter.2.cloned.1.call-done = f32[128,256]{1,0:T(8,128)} async-done(((f32[256,256]{1,0:T(8,128)}), f32[128,256]{1,0:T(8,128)}) %reduce-scatter.2.cloned.1.call-update) | async-done | bytes 131088 | tf_op jit(solution)/shard_map/reduce_scatter | solution.py:53
  (17 shorter events, 0.1 us)
Async XLA Ops:
  6.5 33.1 %all-gather.8.cloned.1.call-start = ((), (), s32[]{:S(2)}) async-start(), calls=%async_computation.3 | async-start | bytes 1310720 | tf_op jit(solution)/shard_map/all_gather | solution.py:47
  7.3 0.9 copy-start.1
  7.3 60.2 %all-gather.10.cloned.1.call-start = ((), (), s32[]{:S(2)}) async-start(), calls=%async_computation.4 | async-start | bytes 1310720 | tf_op jit(solution)/shard_map/all_gather | solution.py:49
  8.0 89.0 %all-gather.6.cloned.1.call-start = ((), (), s32[]{:S(2)}) async-start(), calls=%async_computation.1 | async-start | bytes 1310720 | tf_op jit(solution)/shard_map/all_gather | solution.py:50
  8.2 15.1 %copy-start.4 = (f32[1,2]{1,0:T(1,128)S(1)}, f32[1,2]{1,0:T(1,128)}, u32[]{:S(2)}) copy-start(f32[1,2]{1,0:T(1,128)} %param.9) | copy-start | bytes 28
  8.2 15.7 %copy-start.2 = (bf16[256,256]{1,0:T(8,128)(2,1)S(1)}, bf16[256,256]{1,0:T(8,128)(2,1)}, u32[]{:S(2)}) copy-start(bf16[256,256]{1,0:T(8,128)(2,1)} %param.6) | copy-start | bytes 393220
  35.9 0.7 copy-start.3
  39.6 2.0 %copy-start.7 = (bf16[1,2,1024,256]{3,2,1,0:T(8,128)(2,1)S(1)}, bf16[1,2,1024,256]{3,2,1,0:T(8,128)(2,1)}, u32[]{:S(2)}) copy-start(bf16[1,2,1024,256]{3,2,1,0:T(8,128)(2,1)} %all-gather.8.cloned.1.call-done) | copy-start | bytes 3145732
  45.2 0.7 copy-start.5
  45.2 65.4 %reduce-scatter.2.cloned.1.call-start = ((), (), s32[]{:S(2)}) async-start(), calls=%async_computation.2 | async-start | bytes 393216 | tf_op jit(solution)/shard_map/reduce_scatter | solution.py:53
  67.4 31.1 %copy-start.6 = (bf16[1,2,256,1024]{3,2,1,0:T(8,128)(2,1)S(1)}, bf16[1,2,256,1024]{3,2,1,0:T(8,128)(2,1)}, u32[]{:S(2)}) copy-start(bf16[1,2,256,1024]{3,2,1,0:T(8,128)(2,1)} %all-gather.10.cloned.1.call-done) | copy-start | bytes 3145732
  98.5 1.4 %copy-start.8 = (bf16[2,1024,256]{2,1,0:T(8,128)(2,1)S(1)}, bf16[2,1024,256]{2,1,0:T(8,128)(2,1)}, u32[]{:S(2)}) copy-start(bf16[2,1024,256]{2,1,0:T(8,128)(2,1)} %all-gather.6.cloned.1.call-done) | copy-start | bytes 3145732
  100.3 1.0 copy-start
Sparse Core Ops, SparseCore 0:
  8.9 30.6 all-gather.7
  41.4 25.9 all-gather.9
  69.0 27.9 all-gather.5
  103.5 7.1 reduce-scatter.1
where the time goes:
time: 118 us; the launch traced here: 117 us
  waiting for transfers between devices  61.5 us (52%)
  blocking collectives  27.2 us (23%)
  between operations  13.3 us (11%)
  matrix products  8.97 us (8%)
  local copies, waits for them, and re-layouts  3.23 us (3%)
  other arithmetic  2.91 us (2%)
    all_gather x1, waiting for transfers between devices, per_device(): lax.all_gather(product_local, 'layer', axis=1, tiled=True)  29.5 us
    all_gather x1, waiting for transfers between devices, per_device(): lax.all_gather(guess_local, ('row', 'col'), axis=2, tiled=True)  20.9 us
    all_gather x1, blocking collectives, per_device(): lax.all_gather(intersection, ('row', 'col'), axis=1, tiled=True)  15.1 us
    all_gather x1, blocking collectives, per_device(): lax.all_gather(hamilton, ('row', 'col'), axis=1, tiled=True)  12.1 us
    reduce_scatter x1, waiting for transfers between devices, per_device(): reduced = lax.psum_scatter(contrib, 'pole', scatter_dimension=0, tiled=True)  7.3 us
    dot_general x2, matrix products, fold_terms(): jnp.dot(left_panel[0], piece[0], preferred_element_type=jnp.float32)  3.5 us
  transfers between devices with their start and end apart: 4, of which 4 were waited for; matrix products, arithmetic and copies ran while one was open for 6% of the time, Pallas kernels for 0%

commit v1 on v0

v1 whole, which is shorter than its diff:
```python
import jax
import jax.numpy as jnp
from jax import lax
from jax.experimental import pallas as pl
from jax.experimental.pallas import tpu as pltpu
from jax.sharding import PartitionSpec as P

BLOCK = 128
MESH = pl.DeviceIdType.MESH


def fused(
    layers, rows_axis, cols_axis,
    ham_ref, ovl_ref, guess_ref, poles_ref, weights_ref, keep_ref, out_ref,
    hs, gcol, grow, prod, sysm, mine, red_out, red_in,
    hs_send, hs_recv, gc_send, gc_recv, gr_send, gr_recv, pr_send, pr_recv, rd_send, rd_recv,
):
    spans = rows_axis * cols_axis
    rows, cols = ham_ref.shape
    half = rows // 2
    layer = lax.axis_index("layer")
    row, col, pole = lax.axis_index("row"), lax.axis_index("col"), lax.axis_index("pole")
    span = row * cols_axis + col
    layer_peers = [lax.rem(layer + d, layers) for d in range(1, layers)]
    span_peers = [
        (lax.rem(row + a, rows_axis), lax.rem(col + b, cols_axis))
        for a in range(rows_axis) for b in range(cols_axis) if a or b
    ]

    barrier = pltpu.get_barrier_semaphore()
    for k in layer_peers:
        pl.semaphore_signal(barrier, inc=1, device_id={"layer": k}, device_id_type=MESH)
    for r, c in span_peers:
        pl.semaphore_signal(barrier, inc=1, device_id={"row": r, "col": c}, device_id_type=MESH)
    pl.semaphore_signal(barrier, inc=1, device_id={"pole": 1 - pole}, device_id_type=MESH)
    pl.semaphore_wait(barrier, layers + spans - 1)

    def to_layer(i, k, src, dst, send, recv):
        return pltpu.make_async_remote_copy(
            src_ref=src, dst_ref=dst.at[layer], send_sem=send.at[i], recv_sem=recv.at[layer],
            device_id={"layer": k}, device_id_type=MESH)

    def to_span(i, peer, src, dst, send, recv):
        return pltpu.make_async_remote_copy(
            src_ref=src, dst_ref=dst, send_sem=send.at[i], recv_sem=recv,
            device_id={"row": peer[0], "col": peer[1]}, device_id_type=MESH)

    sends = []

    def go(copy):
        copy.start()
        sends.append(copy)

    for i, k in enumerate(layer_peers):
        go(to_layer(i, k, guess_ref, gcol, gc_send, gc_recv))
    for i, peer in enumerate(span_peers):
        go(to_span(i, peer, ham_ref, hs.at[span, 0], hs_send.at[0], hs_recv.at[0, span]))
        go(to_span(i, peer, ovl_ref, hs.at[span, 1], hs_send.at[1], hs_recv.at[1, span]))
    for i, peer in enumerate(span_peers):
        go(to_span(i, peer, guess_ref, grow.at[span], gr_send, gr_recv.at[span]))

    zr, zi = poles_ref[0, 0], poles_ref[0, 1]
    wr, wi = weights_ref[0, 0], weights_ref[0, 1]

    def put_system(s, ham, ovl):
        ovl = ovl.astype(jnp.float32)
        re = (zr * ovl - ham.astype(jnp.float32)).astype(jnp.bfloat16)
        im = zi * ovl
        pos, neg = im.astype(jnp.bfloat16), (-im).astype(jnp.bfloat16)
        for j in range(cols // rows):
            part = slice(j * rows, (j + 1) * rows)
            n = s * (cols // rows) + j
            sysm[n, :rows, :rows] = re[:, part]
            sysm[n, :rows, rows:] = neg[:, part]
            sysm[n, rows:, :rows] = pos[:, part]
            sysm[n, rows:, rows:] = re[:, part]

    tile_rows, tile_cols = rows // BLOCK, cols // BLOCK

    def masked(value):
        out = []
        for a in range(tile_rows):
            line = []
            for b in range(tile_cols):
                flag = keep_ref[layer * tile_rows + a, span * tile_cols + b].astype(jnp.float32)
                line.append(
                    value[a * BLOCK:(a + 1) * BLOCK, b * BLOCK:(b + 1) * BLOCK] * flag)
            out.append(jnp.concatenate(line, axis=1))
        return jnp.concatenate(out, axis=0)

    put_system(span, ham_ref[...], ovl_ref[...])
    for r, c in span_peers:
        s = r * cols_axis + c
        for j in range(2):
            pltpu.make_async_remote_copy(
                src_ref=hs.at[s, j], dst_ref=hs.at[s, j], send_sem=hs_send.at[j, 0],
                recv_sem=hs_recv.at[j, s], device_id={"row": r, "col": c}, device_id_type=MESH,
            ).wait_recv()
        put_system(s, hs[s, 0], hs[s, 1])

    def got_layer(k, dst, recv, send):
        pltpu.make_async_remote_copy(
            src_ref=dst.at[k], dst_ref=dst.at[k], send_sem=send.at[0],
            recv_sem=recv.at[k], device_id={"layer": k}, device_id_type=MESH,
        ).wait_recv()

    acc = jnp.dot(sysm[layer], guess_ref[...].reshape(2 * rows, cols),
                  preferred_element_type=jnp.float32)
    for d in range(1, layers):
        k = lax.rem(layer + d, layers)
        got_layer(k, gcol, gc_recv, gc_send)
        acc += jnp.dot(sysm[k], gcol[k].reshape(2 * rows, cols),
                       preferred_element_type=jnp.float32)
    pre, pim = masked(acc[:rows]), masked(acc[rows:])
    mine[0] = (wr * pre - wi * pim).astype(jnp.bfloat16)
    mine[1] = (-wi * pre - wr * pim).astype(jnp.bfloat16)

    for i, k in enumerate(layer_peers):
        go(to_layer(i, k, mine, prod, pr_send, pr_recv))

    for r, c in span_peers:
        s = r * cols_axis + c
        pltpu.make_async_remote_copy(
            src_ref=grow.at[s], dst_ref=grow.at[s], send_sem=gr_send.at[0],
            recv_sem=gr_recv.at[s], device_id={"row": r, "col": c}, device_id_type=MESH,
        ).wait_recv()
    grow[span] = guess_ref[...]

    ratio = cols // rows

    def back(k, q):
        if ratio == 1:
            gr, gi = grow[k, 0], grow[k, 1]
        else:
            at = pl.ds(pl.multiple_of(lax.rem(k, ratio) * rows, rows), rows)
            gr, gi = grow[k // ratio, 0, :, at], grow[k // ratio, 1, :, at]
        return (jnp.dot(gr, q[0], preferred_element_type=jnp.float32)
                + jnp.dot(gi, q[1], preferred_element_type=jnp.float32))

    total = back(layer, mine[...])
    for d in range(1, layers):
        k = lax.rem(layer + d, layers)
        got_layer(k, prod, pr_recv, pr_send)
        total += back(k, prod[k])
    own = guess_ref[...].astype(jnp.float32)
    red_out[...] = masked(2.0 * (wr * own[0] - wi * own[1]) - total).reshape(2, half, cols)
    swap = pltpu.make_async_remote_copy(
        src_ref=red_out.at[1 - pole], dst_ref=red_in, send_sem=rd_send, recv_sem=rd_recv,
        device_id={"pole": 1 - pole}, device_id_type=MESH)
    swap.start()
    swap.wait_recv()
    out_ref[...] = red_out[pole] + red_in[...]
    swap.wait_send()
    for copy in sends:
        copy.wait_send()


def solution(mesh):
    layers, rows_axis, cols_axis = (mesh.shape[a] for a in ("layer", "row", "col"))
    spans = rows_axis * cols_axis

    def per_device(hamilton, intersection, guess, poles, weights, keep):
        rows, cols = hamilton.shape
        vmem = pl.BlockSpec(memory_space=pltpu.VMEM)
        smem = pl.BlockSpec(memory_space=pltpu.SMEM)
        bf16, dma = jnp.bfloat16, pltpu.SemaphoreType.DMA

        def kernel(*refs):
            fused(layers, rows_axis, cols_axis, *refs)

        out = pl.pallas_call(
            kernel,
            out_shape=jax.ShapeDtypeStruct((rows // 2, cols), jnp.float32),
            in_specs=[vmem, vmem, vmem, smem, smem, smem],
            out_specs=vmem,
            scratch_shapes=[
                pltpu.VMEM((spans, 2, rows, cols), bf16),
                pltpu.VMEM((layers, 2, rows, cols), bf16),
                pltpu.VMEM((spans, 2, rows, cols), bf16),
                pltpu.VMEM((layers, 2, rows, cols), bf16),
                pltpu.VMEM((layers, 2 * rows, 2 * rows), bf16),
                pltpu.VMEM((2, rows, cols), bf16),
                pltpu.VMEM((2, rows // 2, cols), jnp.float32),
                pltpu.VMEM((rows // 2, cols), jnp.float32),
                dma((2, spans)), dma((2, spans)),
                dma((layers,)), dma((layers,)),
                dma((spans,)), dma((spans,)),
                dma((layers,)), dma((layers,)),
                dma, dma,
            ],
            compiler_params=pltpu.CompilerParams(
                collective_id=0, has_side_effects=True, vmem_limit_bytes=56 * 2**20),
            cost_estimate=pl.CostEstimate(
                flops=12 * rows * rows * layers * cols, bytes_accessed=16 * rows * cols,
                transcendentals=0),
        )(hamilton, intersection, guess[0], poles, weights, keep[0])
        return out.reshape(1, 1, rows // 2, cols)

    in_specs = (
        P("layer", ("row", "col")),
        P("layer", ("row", "col")),
        P("pole", None, "layer", ("row", "col")),
        P("pole", None),
        P("pole", None),
        P("pole", None, None),
    )
    return jax.shard_map(
        per_device, mesh=mesh, in_specs=in_specs,
        out_specs=P("layer", "pole", None, ("row", "col")), check_vma=False,
    )
```

time: 118 us -> 55.7 us (0.47)
  the two profiles are of different devices: /device:TPU:0 before, /device:TPU:31 now
where the time goes in v1:
time: 55.7 us; the launch traced here: 55.6 us
  Pallas kernels  54 us (97%)
  local copies, waits for them, and re-layouts  1.57 us (3%)
    pallas_call x1, Pallas kernels, per_device(): pl.pallas_call(kernel, out_shape=jax.ShapeDtypeStruct((rows // 2, cols),...  54 us
    unnamed x1, local copies, waits for them, and re-layouts  1.57 us

profile of v1, /device:TPU:31, one launch (start us, length us, event | category | flops | bytes accessed | tf_op | source)
XLA Modules:
  0.0 55.6 jit_solution(3505592811946705111)
XLA Ops:
  0.0 54.0 %shard_map.64 = f32[128,256]{1,0:T(8,128)} custom-call(bf16[256,256]{1,0:T(8,128)(2,1)} %refs_0_.1, bf16[256,256]{1,0:T(8,128)(2,1)} %refs_1_.1, bf16[2,256,256]{2,1,0:T(8,128)(2,1)} %bitcast.4, f32[1,2]{1,0:T(1,128)} %refs_3_.1, f32[1,2]{1,0:T(1,128)} %refs_4_.1, s32[8,8]{1,0:T(8,128)} %bitcast.5), custom_call_target="tpu_custom_call" | custom-call | flops 805306368 | bytes 1048576 | tf_op jit(solution)/shard_map/pallas_call | solution.py:171
  54.0 1.6 %copy.8 = f32[1,1,128,256]{3,2,1,0:T(8,128)} copy(f32[1,1,128,256]{3,2,1,0:T(8,128)} %bitcast.3) | data formatting | bytes 262144

commit v2 on v1

--- a/solution.py
+++ b/solution.py
@@ -155,6 +155,240 @@
         copy.wait_send()
 
 
+def paired(
+    ham_ref, ovl_ref, guess_ref, poles_ref, weights_ref, keep_ref, out_ref,
+    hs, gcol, rowg, qb, sysm, acc, red_out, red_in, pair_out, pair_in,
+    z_send, z_recv, hs_send, hs_recv, sib_send, sib_recv, y_send, y_recv, x_send, x_recv,
+    q_send, q_recv, rd_send, rd_recv, pt_send, pt_recv,
+):
+    layers = 4
+    rows, cols = ham_ref.shape
+    half = rows // 2
+    layer = lax.axis_index("layer")
+    row, col, pole = lax.axis_index("row"), lax.axis_index("col"), lax.axis_index("pole")
+    span = row * 2 + col
+    top = layer // 2
+    odd = lax.rem(layer, 2)
+    partner = lax.rem(layer + 2, 4)
+    beside = 2 * top + 1 - odd
+    is_root = row == top
+    others = [(lax.rem(row + a, 2), lax.rem(col + b, 2)) for a, b in ((1, 0), (0, 1), (1, 1))]
+
+    barrier = pltpu.get_barrier_semaphore()
+    for d in range(1, layers):
+        pl.semaphore_signal(
+            barrier, inc=1, device_id={"layer": lax.rem(layer + d, layers)}, device_id_type=MESH)
+    for r, c in others:
+        pl.semaphore_signal(barrier, inc=1, device_id={"row": r, "col": c}, device_id_type=MESH)
+    pl.semaphore_signal(barrier, inc=1, device_id={"pole": 1 - pole}, device_id_type=MESH)
+    pl.semaphore_wait(barrier, 7)
+
+    def remote(src, dst, send, recv, where):
+        return pltpu.make_async_remote_copy(
+            src_ref=src, dst_ref=dst, send_sem=send, recv_sem=recv,
+            device_id=where, device_id_type=MESH)
+
+    def zcopy(i, src, slot, k):
+        return remote(src, gcol.at[slot], z_send.at[i], z_recv.at[slot], {"layer": k})
+
+    @pl.when(layer < 3)
+    def _():
+        zcopy(0, guess_ref, layer, layer + 1).start()
+
+    @pl.when(layer > 0)
+    def _():
+        zcopy(1, guess_ref, layer, layer - 1).start()
+
+    for j in range(2):
+        hs[span, j, 0] = ham_ref[j * half:(j + 1) * half]
+        hs[span, j, 1] = ovl_ref[j * half:(j + 1) * half]
+    hs_out = [
+        remote(hs.at[span, pole], hs.at[span, pole], hs_send.at[i], hs_recv.at[span],
+               {"row": r, "col": c})
+        for i, (r, c) in enumerate(others)
+    ]
+    for copy in hs_out:
+        copy.start()
+
+    def ycopy(j):
+        return remote(rowg.at[j, col], rowg.at[j, col], y_send.at[j], y_recv.at[j],
+                      {"row": 1 - row})
+
+    def xcopy(j):
+        return remote(rowg.at[j, col], rowg.at[j, col], x_send.at[j], x_recv.at[j],
+                      {"col": 1 - col})
+
+    def xgot(j):
+        remote(rowg.at[j, 1 - col], rowg.at[j, 1 - col], x_send.at[j], x_recv.at[j],
+               {"col": 1 - col}).wait_recv()
+
+    @pl.when(is_root)
+    def _():
+        rowg[0, col] = guess_ref[...]
+        ycopy(0).start()
+        xcopy(0).start()
+
+    zr, zi = poles_ref[0, 0], poles_ref[0, 1]
+    wr, wi = weights_ref[0, 0], weights_ref[0, 1]
+
+    def put_system(s):
+        for j in range(2):
+            ovl = hs[s, j, 1].astype(jnp.float32)
+            re = (zr * ovl - hs[s, j, 0].astype(jnp.float32)).astype(jnp.bfloat16)
+            im = zi * ovl
+            upper, lower = slice(j * half, (j + 1) * half), slice(rows + j * half, rows + (j + 1) * half)
+            sysm[s, upper, :rows] = re
+            sysm[s, upper, rows:] = (-im).astype(jnp.bfloat16)
+            sysm[s, lower, :rows] = im.astype(jnp.bfloat16)
+            sysm[s, lower, rows:] = re
+
+    put_system(span)
+    shared = []
+    for i, (r, c) in enumerate(others):
+        s = r * 2 + c
+        remote(hs.at[s, pole], hs.at[s, pole], hs_send.at[i], hs_recv.at[s],
+               {"row": r, "col": c}).wait_recv()
+        copy = remote(hs.at[s, pole], hs.at[s, pole], sib_send.at[s], sib_recv.at[s],
+                      {"pole": 1 - pole})
+        copy.start()
+        shared.append(copy)
+
+    def arrive(d):
+        @pl.when(layer - d >= 0)
+        def _():
+            k = layer - d
+            zcopy(0, gcol.at[k], k, k).wait_recv()
+
+            @pl.when(layer < 3)
+            def _():
+                zcopy(2 * d, gcol.at[k], k, layer + 1).start()
+
+        @pl.when(layer + d <= 3)
+        def _():
+            k = layer + d
+            zcopy(0, gcol.at[k], k, k).wait_recv()
+
+            @pl.when(layer > 0)
+            def _():
+                zcopy(2 * d + 1, gcol.at[k], k, layer - 1).start()
+
+    def fold(d):
+        for k, there in ((layer - d, layer - d >= 0), (layer + d, layer + d <= 3)):
+            @pl.when(there)
+            def _():
+                acc[...] += jnp.dot(sysm[k], gcol[k].reshape(2 * rows, cols),
+                                    preferred_element_type=jnp.float32)
+
+    arrive(1)
+    for r, c in others:
+        s = r * 2 + c
+        remote(hs.at[s, 1 - pole], hs.at[s, 1 - pole], sib_send.at[s], sib_recv.at[s],
+               {"pole": 1 - pole}).wait_recv()
+        put_system(s)
+    acc[...] = jnp.dot(sysm[layer], guess_ref[...].reshape(2 * rows, cols),
+                       preferred_element_type=jnp.float32)
+    fold(1)
+    arrive(2)
+
+    @pl.when(is_root)
+    def _():
+        rowg[1, col] = gcol[partner]
+        ycopy(1).start()
+        xcopy(1).start()
+
+    @pl.when(jnp.logical_not(is_root))
+    def _():
+        ycopy(0).wait_recv()
+        xcopy(0).start()
+
+    fold(2)
+    arrive(3)
+    fold(3)
+
+    tiles = rows // BLOCK
+
+    def masked(at, value):
+        out = []
+        for a in range(tiles):
+            line = []
+            for b in range(tiles):
+                flag = keep_ref[at * tiles + a, span * tiles + b].astype(jnp.float32)
+                line.append(
+                    value[a * BLOCK:(a + 1) * BLOCK, b * BLOCK:(b + 1) * BLOCK] * flag)
+            out.append(jnp.concatenate(line, axis=1))
+        return jnp.concatenate(out, axis=0)
+
+    pre, pim = masked(layer, acc[:rows]), masked(layer, acc[rows:])
+    qb[odd, 0] = (wr * pre - wi * pim).astype(jnp.bfloat16)
+    qb[odd, 1] = (-wi * pre - wr * pim).astype(jnp.bfloat16)
+    give = remote(qb.at[odd], qb.at[odd], q_send, q_recv, {"layer": beside})
+    give.start()
+
+    @pl.when(jnp.logical_not(is_root))
+    def _():
+        ycopy(1).wait_recv()
+        xcopy(1).start()
+
+    own = guess_ref[...].astype(jnp.float32)
+    xgot(0)
+    xgot(1)
+
+    def part(j, s):
+        return (jnp.dot(rowg[j, s, 0], qb[s, 0], preferred_element_type=jnp.float32)
+                + jnp.dot(rowg[j, s, 1], qb[s, 1], preferred_element_type=jnp.float32))
+
+    far, near = part(1, odd), part(0, odd)
+    remote(qb.at[1 - odd], qb.at[1 - odd], q_send, q_recv, {"layer": beside}).wait_recv()
+
+    def swap(j):
+        return remote(red_out.at[j, 1 - pole], red_in.at[j], rd_send.at[j], rd_recv.at[j],
+                      {"pole": 1 - pole})
+
+    far = far + part(1, 1 - odd)
+    red_out[1] = masked(partner, far).reshape(2, half, cols)
+    swap(1).start()
+    near = near + part(0, 1 - odd)
+    red_out[0] = masked(layer, 2.0 * (wr * own[0] - wi * own[1]) - near).reshape(2, half, cols)
+    swap(0).start()
+    swap(1).wait_recv()
+    pair_out[...] = (red_out[1, pole] + red_in[1]).astype(jnp.bfloat16)
+    last = remote(pair_out, pair_in, pt_send, pt_recv, {"layer": partner})
+    last.start()
+    swap(0).wait_recv()
+    near_sum = red_out[0, pole] + red_in[0]
+    last.wait_recv()
+    out_ref[...] = near_sum - pair_in[...].astype(jnp.float32)
+
+    @pl.when(layer < 3)
+    def _():
+        zcopy(0, guess_ref, layer, layer + 1).wait_send()
+
+    @pl.when(layer > 0)
+    def _():
+        zcopy(1, guess_ref, layer, layer - 1).wait_send()
+
+    for d in range(1, layers):
+        @pl.when((layer - d >= 0) & (layer < 3))
+        def _():
+            zcopy(2 * d, gcol.at[layer - d], layer - d, layer + 1).wait_send()
+
+        @pl.when((layer + d <= 3) & (layer > 0))
+        def _():
+            zcopy(2 * d + 1, gcol.at[layer + d], layer + d, layer - 1).wait_send()
+
+    for copy in hs_out + shared:
+        copy.wait_send()
+    for j in range(2):
+        @pl.when(is_root)
+        def _():
+            ycopy(j).wait_send()
+
+        xcopy(j).wait_send()
+        swap(j).wait_send()
+    give.wait_send()
+    last.wait_send()
+
+
 def solution(mesh):
     layers, rows_axis, cols_axis = (mesh.shape[a] for a in ("layer", "row", "col"))
     spans = rows_axis * cols_axis
@@ -165,15 +399,37 @@
         smem = pl.BlockSpec(memory_space=pltpu.SMEM)
         bf16, dma = jnp.bfloat16, pltpu.SemaphoreType.DMA
 
+        in_pairs = layers == 4 and rows_axis == 2 and cols_axis == 2 and rows == cols
+
         def kernel(*refs):
-            fused(layers, rows_axis, cols_axis, *refs)
+            if in_pairs:
+                paired(*refs)
+            else:
+                fused(layers, rows_axis, cols_axis, *refs)
+
+        half = rows // 2
+        pair_scratch = [
+            pltpu.VMEM((4, 2, 2, half, cols), bf16),
+            pltpu.VMEM((4, 2, rows, cols), bf16),
+            pltpu.VMEM((2, 2, 2, rows, cols), bf16),
+            pltpu.VMEM((2, 2, rows, cols), bf16),
+            pltpu.VMEM((4, 2 * rows, 2 * rows), bf16),
+            pltpu.VMEM((2 * rows, cols), jnp.float32),
+            pltpu.VMEM((2, 2, half, cols), jnp.float32),
+            pltpu.VMEM((2, half, cols), jnp.float32),
+            pltpu.VMEM((half, cols), bf16),
+            pltpu.VMEM((half, cols), bf16),
+            dma((8,)), dma((4,)), dma((3,)), dma((4,)), dma((4,)), dma((4,)),
+            dma((2,)), dma((2,)), dma((2,)), dma((2,)),
+            dma, dma, dma((2,)), dma((2,)), dma, dma,
+        ]
 
         out = pl.pallas_call(
             kernel,
             out_shape=jax.ShapeDtypeStruct((rows // 2, cols), jnp.float32),
             in_specs=[vmem, vmem, vmem, smem, smem, smem],
             out_specs=vmem,
-            scratch_shapes=[
+            scratch_shapes=pair_scratch if in_pairs else [
                 pltpu.VMEM((spans, 2, rows, cols), bf16),
                 pltpu.VMEM((layers, 2, rows, cols), bf16),
                 pltpu.VMEM((spans, 2, rows, cols), bf16),

time: 55.7 us -> 43.6 us (0.78)
  the two profiles are of different devices: /device:TPU:31 before, /device:TPU:0 now
where the time goes in v2:
time: 43.6 us; the launch traced here: 43.4 us
  Pallas kernels  41.8 us (96%)
  local copies, waits for them, and re-layouts  1.57 us (4%)
    pallas_call x1, Pallas kernels, per_device(): pl.pallas_call(kernel, out_shape=jax.ShapeDtypeStruct((rows // 2, cols),...  41.8 us
    unnamed x1, local copies, waits for them, and re-layouts  1.57 us

profile of v2, /device:TPU:0, one launch (start us, length us, event | category | flops | bytes accessed | tf_op | source)
XLA Modules:
  0.0 43.4 jit_solution(10596244431511267620)
XLA Ops:
  0.0 41.8 %shard_map.64 = f32[128,256]{1,0:T(8,128)} custom-call(bf16[256,256]{1,0:T(8,128)(2,1)} %refs_0_.1, bf16[256,256]{1,0:T(8,128)(2,1)} %refs_1_.1, bf16[2,256,256]{2,1,0:T(8,128)(2,1)} %bitcast.4, f32[1,2]{1,0:T(1,128)} %refs_3_.1, f32[1,2]{1,0:T(1,128)} %refs_4_.1, s32[8,8]{1,0:T(8,128)} %bitcast.5), custom_call_target="tpu_custom_call" | custom-call | flops 805306368 | bytes 1048576 | tf_op jit(solution)/shard_map/pallas_call | solution.py:427
  41.8 1.6 %copy.8 = f32[1,1,128,256]{3,2,1,0:T(8,128)} copy(f32[1,1,128,256]{3,2,1,0:T(8,128)} %bitcast.3) | data formatting | bytes 262144

commit v3 on v1

--- a/solution.py
+++ b/solution.py
@@ -155,6 +155,271 @@
         copy.wait_send()
 
 
+def paired(
+    ham_ref, ovl_ref, guess_ref, poles_ref, weights_ref, keep_ref, out_ref,
+    hs, gcol, rowg, qb, sysm, acc, red_out, red_in, pair_out, pair_in,
+    z_send, z_recv, hs_send, hs_recv, sib_send, sib_recv, y_send, y_recv, x_send, x_recv,
+    q_send, q_recv, rd_send, rd_recv, pt_send, pt_recv,
+):
+    layers = 4
+    rows, cols = ham_ref.shape
+    half = rows // 2
+    layer = lax.axis_index("layer")
+    row, col, pole = lax.axis_index("row"), lax.axis_index("col"), lax.axis_index("pole")
+    span = row * 2 + col
+    top = layer // 2
+    odd = lax.rem(layer, 2)
+    partner = lax.rem(layer + 2, 4)
+    beside = 2 * top + 1 - odd
+    is_root = row == top
+    others = [(lax.rem(row + a, 2), lax.rem(col + b, 2)) for a, b in ((1, 0), (0, 1), (1, 1))]
+
+    barrier = pltpu.get_barrier_semaphore()
+    for d in range(1, layers):
+        pl.semaphore_signal(
+            barrier, inc=1, device_id={"layer": lax.rem(layer + d, layers)}, device_id_type=MESH)
+    for r, c in others:
+        pl.semaphore_signal(barrier, inc=1, device_id={"row": r, "col": c}, device_id_type=MESH)
+    pl.semaphore_signal(barrier, inc=1, device_id={"pole": 1 - pole}, device_id_type=MESH)
+    pl.semaphore_wait(barrier, 7)
+
+    def remote(src, dst, send, recv, where):
+        return pltpu.make_async_remote_copy(
+            src_ref=src, dst_ref=dst, send_sem=send, recv_sem=recv,
+            device_id=where, device_id_type=MESH)
+
+    width = cols // 2
+    chunk = [slice(h * width, (h + 1) * width) for h in range(2)]
+
+    def zcopy(i, h, src, slot, k):
+        return remote(src.at[:, :, chunk[h]], gcol.at[slot, :, :, chunk[h]],
+                      z_send.at[i, h], z_recv.at[slot, h], {"layer": k})
+
+    def send_own(h):
+        @pl.when(layer < 3)
+        def _():
+            zcopy(0, h, guess_ref, layer, layer + 1).start()
+
+        @pl.when(layer > 0)
+        def _():
+            zcopy(1, h, guess_ref, layer, layer - 1).start()
+
+    send_own(0)
+    send_own(1)
+
+    for j in range(2):
+        hs[span, j, 0] = ham_ref[j * half:(j + 1) * half]
+        hs[span, j, 1] = ovl_ref[j * half:(j + 1) * half]
+    hs_out = [
+        remote(hs.at[span, pole], hs.at[span, pole], hs_send.at[i], hs_recv.at[span],
+               {"row": r, "col": c})
+        for i, (r, c) in enumerate(others)
+    ]
+    for copy in hs_out:
+        copy.start()
+
+    def ycopy(j, h):
+        part = rowg.at[j, col, :, :, chunk[h]]
+        return remote(part, part, y_send.at[j, h], y_recv.at[j, h], {"row": 1 - row})
+
+    def xcopy(j, h):
+        part = rowg.at[j, col, :, :, chunk[h]]
+        return remote(part, part, x_send.at[j, h], x_recv.at[j, h], {"col": 1 - col})
+
+    def xgot(j, h):
+        part = rowg.at[j, 1 - col, :, :, chunk[h]]
+        remote(part, part, x_send.at[j, h], x_recv.at[j, h], {"col": 1 - col}).wait_recv()
+
+    def relay(j, h):
+        @pl.when(jnp.logical_not(is_root))
+        def _():
+            ycopy(j, h).wait_recv()
+            xcopy(j, h).start()
+
+    @pl.when(is_root)
+    def _():
+        rowg[0, col] = guess_ref[...]
+        for h in range(2):
+            ycopy(0, h).start()
+            xcopy(0, h).start()
+
+    zr, zi = poles_ref[0, 0], poles_ref[0, 1]
+    wr, wi = weights_ref[0, 0], weights_ref[0, 1]
+
+    def put_system(s):
+        for j in range(2):
+            ovl = hs[s, j, 1].astype(jnp.float32)
+            re = (zr * ovl - hs[s, j, 0].astype(jnp.float32)).astype(jnp.bfloat16)
+            im = zi * ovl
+            upper, lower = slice(j * half, (j + 1) * half), slice(rows + j * half, rows + (j + 1) * half)
+            sysm[s, upper, :rows] = re
+            sysm[s, upper, rows:] = (-im).astype(jnp.bfloat16)
+            sysm[s, lower, :rows] = im.astype(jnp.bfloat16)
+            sysm[s, lower, rows:] = re
+
+    put_system(span)
+    def arrive(d, h):
+        @pl.when(layer - d >= 0)
+        def _():
+            k = layer - d
+            zcopy(0, h, gcol.at[k], k, k).wait_recv()
+
+            @pl.when(layer < 3)
+            def _():
+                zcopy(2 * d, h, gcol.at[k], k, layer + 1).start()
+
+        @pl.when(layer + d <= 3)
+        def _():
+            k = layer + d
+            zcopy(0, h, gcol.at[k], k, k).wait_recv()
+
+            @pl.when(layer > 0)
+            def _():
+                zcopy(2 * d + 1, h, gcol.at[k], k, layer - 1).start()
+
+    def fold(d, h):
+        for k, there in ((layer - d, layer - d >= 0), (layer + d, layer + d <= 3)):
+            @pl.when(there)
+            def _():
+                acc[:, chunk[h]] += jnp.dot(
+                    sysm[k], gcol[k, :, :, chunk[h]].reshape(2 * rows, width),
+                    preferred_element_type=jnp.float32)
+
+    def spread(h):
+        @pl.when(is_root)
+        def _():
+            rowg[1, col, :, :, chunk[h]] = gcol[partner, :, :, chunk[h]]
+            ycopy(1, h).start()
+            xcopy(1, h).start()
+
+    tiles = rows // BLOCK
+
+    def masked(at, h, value):
+        per = width // BLOCK
+        out = []
+        for a in range(tiles):
+            line = []
+            for b in range(per):
+                flag = keep_ref[at * tiles + a, span * tiles + h * per + b].astype(jnp.float32)
+                line.append(
+                    value[a * BLOCK:(a + 1) * BLOCK, b * BLOCK:(b + 1) * BLOCK] * flag)
+            out.append(jnp.concatenate(line, axis=1))
+        return jnp.concatenate(out, axis=0)
+
+    def give(slot, h):
+        part = qb.at[slot, :, :, chunk[h]]
+        return remote(part, part, q_send.at[h], q_recv.at[h], {"layer": beside})
+
+    def product(h):
+        pre = masked(layer, h, acc[:rows, chunk[h]])
+        pim = masked(layer, h, acc[rows:, chunk[h]])
+        qb[odd, 0, :, chunk[h]] = (wr * pre - wi * pim).astype(jnp.bfloat16)
+        qb[odd, 1, :, chunk[h]] = (-wi * pre - wr * pim).astype(jnp.bfloat16)
+        give(odd, h).start()
+
+    arrive(1, 0)
+    arrive(2, 0)
+    spread(0)
+    shared = []
+    for i, (r, c) in enumerate(others):
+        s = r * 2 + c
+        remote(hs.at[s, pole], hs.at[s, pole], hs_send.at[i], hs_recv.at[s],
+               {"row": r, "col": c}).wait_recv()
+        copy = remote(hs.at[s, pole], hs.at[s, pole], sib_send.at[s], sib_recv.at[s],
+                      {"pole": 1 - pole})
+        copy.start()
+        shared.append(copy)
+    for r, c in others:
+        s = r * 2 + c
+        remote(hs.at[s, 1 - pole], hs.at[s, 1 - pole], sib_send.at[s], sib_recv.at[s],
+               {"pole": 1 - pole}).wait_recv()
+        put_system(s)
+    arrive(1, 1)
+    acc[...] = jnp.dot(sysm[layer], guess_ref[...].reshape(2 * rows, cols),
+                       preferred_element_type=jnp.float32)
+    fold(1, 0)
+    fold(2, 0)
+    arrive(3, 0)
+    fold(3, 0)
+    product(0)
+    relay(0, 0)
+    arrive(2, 1)
+    spread(1)
+    relay(0, 1)
+    fold(1, 1)
+    fold(2, 1)
+    relay(1, 0)
+    arrive(3, 1)
+    fold(3, 1)
+    product(1)
+    relay(1, 1)
+
+    for j in range(2):
+        for h in range(2):
+            xgot(j, h)
+
+    def part(j, s, h):
+        return (jnp.dot(rowg[j, s, 0], qb[s, 0, :, chunk[h]], preferred_element_type=jnp.float32)
+                + jnp.dot(rowg[j, s, 1], qb[s, 1, :, chunk[h]], preferred_element_type=jnp.float32))
+
+    def swap(j, h):
+        return remote(red_out.at[j, 1 - pole, :, chunk[h]], red_in.at[j, :, chunk[h]],
+                      rd_send.at[j, h], rd_recv.at[j, h], {"pole": 1 - pole})
+
+    def last(h):
+        return remote(pair_out.at[:, chunk[h]], pair_in.at[:, chunk[h]],
+                      pt_send.at[h], pt_recv.at[h], {"layer": partner})
+
+    for h in range(2):
+        give(1 - odd, h).wait_recv()
+        far = masked(partner, h, part(1, 0, h) + part(1, 1, h))
+        red_out[1, :, :, chunk[h]] = far.reshape(2, half, width)
+        swap(1, h).start()
+        own = guess_ref[:, :, chunk[h]].astype(jnp.float32)
+        near = 2.0 * (wr * own[0] - wi * own[1]) - part(0, 0, h) - part(0, 1, h)
+        red_out[0, :, :, chunk[h]] = masked(layer, h, near).reshape(2, half, width)
+        swap(0, h).start()
+        swap(1, h).wait_recv()
+        pair_out[:, chunk[h]] = (
+            red_out[1, pole, :, chunk[h]] + red_in[1, :, chunk[h]]).astype(jnp.bfloat16)
+        last(h).start()
+    for h in range(2):
+        swap(0, h).wait_recv()
+        last(h).wait_recv()
+        out_ref[:, chunk[h]] = (red_out[0, pole, :, chunk[h]] + red_in[0, :, chunk[h]]
+                                - pair_in[:, chunk[h]].astype(jnp.float32))
+
+    for h in range(2):
+        @pl.when(layer < 3)
+        def _():
+            zcopy(0, h, guess_ref, layer, layer + 1).wait_send()
+
+        @pl.when(layer > 0)
+        def _():
+            zcopy(1, h, guess_ref, layer, layer - 1).wait_send()
+
+        for d in range(1, layers):
+            @pl.when((layer - d >= 0) & (layer < 3))
+            def _():
+                zcopy(2 * d, h, gcol.at[layer - d], layer - d, layer + 1).wait_send()
+
+            @pl.when((layer + d <= 3) & (layer > 0))
+            def _():
+                zcopy(2 * d + 1, h, gcol.at[layer + d], layer + d, layer - 1).wait_send()
+
+        for j in range(2):
+            @pl.when(is_root)
+            def _():
+                ycopy(j, h).wait_send()
+
+            xcopy(j, h).wait_send()
+            swap(j, h).wait_send()
+        give(odd, h).wait_send()
+        last(h).wait_send()
+    for copy in hs_out + shared:
+        copy.wait_send()
+
+
 def solution(mesh):
     layers, rows_axis, cols_axis = (mesh.shape[a] for a in ("layer", "row", "col"))
     spans = rows_axis * cols_axis
@@ -165,15 +430,37 @@
         smem = pl.BlockSpec(memory_space=pltpu.SMEM)
         bf16, dma = jnp.bfloat16, pltpu.SemaphoreType.DMA
 
+        in_pairs = layers == 4 and rows_axis == 2 and cols_axis == 2 and rows == cols
+
         def kernel(*refs):
-            fused(layers, rows_axis, cols_axis, *refs)
+            if in_pairs:
+                paired(*refs)
+            else:
+                fused(layers, rows_axis, cols_axis, *refs)
+
+        half = rows // 2
+        pair_scratch = [
+            pltpu.VMEM((4, 2, 2, half, cols), bf16),
+            pltpu.VMEM((4, 2, rows, cols), bf16),
+            pltpu.VMEM((2, 2, 2, rows, cols), bf16),
+            pltpu.VMEM((2, 2, rows, cols), bf16),
+            pltpu.VMEM((4, 2 * rows, 2 * rows), bf16),
+            pltpu.VMEM((2 * rows, cols), jnp.float32),
+            pltpu.VMEM((2, 2, half, cols), jnp.float32),
+            pltpu.VMEM((2, half, cols), jnp.float32),
+            pltpu.VMEM((half, cols), bf16),
+            pltpu.VMEM((half, cols), bf16),
+            dma((8, 2)), dma((4, 2)), dma((3,)), dma((4,)), dma((4,)), dma((4,)),
+            dma((2, 2)), dma((2, 2)), dma((2, 2)), dma((2, 2)),
+            dma((2,)), dma((2,)), dma((2, 2)), dma((2, 2)), dma((2,)), dma((2,)),
+        ]
 
         out = pl.pallas_call(
             kernel,
             out_shape=jax.ShapeDtypeStruct((rows // 2, cols), jnp.float32),
             in_specs=[vmem, vmem, vmem, smem, smem, smem],
             out_specs=vmem,
-            scratch_shapes=[
+            scratch_shapes=pair_scratch if in_pairs else [
                 pltpu.VMEM((spans, 2, rows, cols), bf16),
                 pltpu.VMEM((layers, 2, rows, cols), bf16),
                 pltpu.VMEM((spans, 2, rows, cols), bf16),

time: 55.7 us -> 40.4 us (0.73)
  the two profiles are of different devices: /device:TPU:31 before, /device:TPU:0 now
where the time goes in v3:
time: 40.4 us; the launch traced here: 40.3 us
  Pallas kernels  38.7 us (96%)
  local copies, waits for them, and re-layouts  1.57 us (4%)
    pallas_call x1, Pallas kernels, per_device(): pl.pallas_call(kernel, out_shape=jax.ShapeDtypeStruct((rows // 2, cols),...  38.7 us
    unnamed x1, local copies, waits for them, and re-layouts  1.57 us

profile of v3, /device:TPU:0, one launch (start us, length us, event | category | flops | bytes accessed | tf_op | source)
XLA Modules:
  0.0 40.3 jit_solution(8338321025262418365)
XLA Ops:
  0.0 38.7 %shard_map.64 = f32[128,256]{1,0:T(8,128)} custom-call(bf16[256,256]{1,0:T(8,128)(2,1)} %refs_0_.1, bf16[256,256]{1,0:T(8,128)(2,1)} %refs_1_.1, bf16[2,256,256]{2,1,0:T(8,128)(2,1)} %bitcast.4, f32[1,2]{1,0:T(1,128)} %refs_3_.1, f32[1,2]{1,0:T(1,128)} %refs_4_.1, s32[8,8]{1,0:T(8,128)} %bitcast.5), custom_call_target="tpu_custom_call" | custom-call | flops 805306368 | bytes 1048576 | tf_op jit(solution)/shard_map/pallas_call | solution.py:458
  38.7 1.6 %copy.8 = f32[1,1,128,256]{3,2,1,0:T(8,128)} copy(f32[1,1,128,256]{3,2,1,0:T(8,128)} %bitcast.3) | data formatting | bytes 262144

commit v4 on v3

--- a/solution.py
+++ b/solution.py
@@ -339,13 +339,13 @@
                        preferred_element_type=jnp.float32)
     fold(1, 0)
     fold(2, 0)
+    relay(0, 0)
     arrive(3, 0)
     fold(3, 0)
     product(0)
-    relay(0, 0)
+    relay(0, 1)
     arrive(2, 1)
     spread(1)
-    relay(0, 1)
     fold(1, 1)
     fold(2, 1)
     relay(1, 0)

time: 40.4 us -> 40.4 us (level)
  no operation moved by 1% of the time
where the time goes in v4:
time: 40.4 us; the launch traced here: 40.3 us
  Pallas kernels  38.7 us (96%)
  local copies, waits for them, and re-layouts  1.57 us (4%)
    pallas_call x1, Pallas kernels, per_device(): pl.pallas_call(kernel, out_shape=jax.ShapeDtypeStruct((rows // 2, cols),...  38.7 us
    unnamed x1, local copies, waits for them, and re-layouts  1.57 us

profile of v4, /device:TPU:0, one launch (start us, length us, event | category | flops | bytes accessed | tf_op | source)
XLA Modules:
  0.0 40.3 jit_solution(18304215431466845092)
XLA Ops:
  0.0 38.7 %shard_map.64 = f32[128,256]{1,0:T(8,128)} custom-call(bf16[256,256]{1,0:T(8,128)(2,1)} %refs_0_.1, bf16[256,256]{1,0:T(8,128)(2,1)} %refs_1_.1, bf16[2,256,256]{2,1,0:T(8,128)(2,1)} %bitcast.4, f32[1,2]{1,0:T(1,128)} %refs_3_.1, f32[1,2]{1,0:T(1,128)} %refs_4_.1, s32[8,8]{1,0:T(8,128)} %bitcast.5), custom_call_target="tpu_custom_call" | custom-call | flops 805306368 | bytes 1048576 | tf_op jit(solution)/shard_map/pallas_call | solution.py:458
  38.7 1.6 %copy.8 = f32[1,1,128,256]{3,2,1,0:T(8,128)} copy(f32[1,1,128,256]{3,2,1,0:T(8,128)} %bitcast.3) | data formatting | bytes 262144
